TPU v7x, 512 devices: a whole 4x8x8 slice. The times are simulated.
512 devices in a mesh: shard: 64 (over x, y, core), rep: 8 (over z).
Axes of the slice: x: 4, y: 8, z: 8, core: 2. Of those that a mesh axis runs over, the one named last changes fastest.
Arguments:
- hidden_acts: bfloat16 [8, 16384, 128], P('rep', 'shard'), may hold values from -6 to 6
- out_grads: bfloat16 [8, 16384, 6144], P('rep', 'shard'), may hold values from -16 to 16
- momentum: float32 [8, 192, 4096], P('rep', 'shard'), may hold values from -6 to 6
- weight_tiles: bfloat16 [192, 4096], P('shard'), may hold values from -1.5 to 1.5
- kept_ids: int32 [8, 192, 4], P('rep', 'shard'), may hold values from 0 to 31, as said below
- kept_counts: int32 [8, 192], P('rep', 'shard'), may hold values from 1 to 4, as said below
Outputs:
- weight_next: bfloat16 [192, 4096], replicated
- momentum_next: float32 [8, 192, 4096], P('rep', 'shard')
Inputs may be any that keep to these rules, and one draw needn't show every extreme that they name: `kept_ids`: the 4 block numbers of one replica's tile are distinct. `kept_counts`: every replica keeps all 4 blocks in at least one tile.
All inputs are finite; a program needn't handle non-finite values.
Results may differ from a plain program's by a relative error of at most 0.007.
Values may be sent and summed in bfloat16 or wider, within the bound.
A program may use at most 64 MiB of HBM per device.

v0:
```python
import math

import jax
import jax.numpy as jnp
from jax import lax
from jax.sharding import PartitionSpec as P

TILE = 64
BROWS = 8
BCOLS = 16
BLOCKS = 32
TILE_SQ = 4096


MOMENTUM_DECAY = 0.9
STEP_FACTOR = 2.0
PRECISE = lax.Precision.HIGHEST


def cosine_basis(basis_order):
    freq_rows = jnp.arange(basis_order).astype(jnp.float32)[:, None]
    sample_cols = jnp.arange(basis_order).astype(jnp.float32)[None, :]
    raw_basis = jnp.cos(math.pi * (2.0 * sample_cols + 1.0) * freq_rows / (2.0 * basis_order))
    norm_scale = jnp.where(
        freq_rows == 0.0, math.sqrt(1.0 / basis_order), math.sqrt(2.0 / basis_order)
    )
    return raw_basis * norm_scale


def to_tiles(grad_mat, tile_size):
    row_count, mat_width = grad_mat.shape
    shaped = grad_mat.reshape(row_count // tile_size, tile_size, mat_width // tile_size, tile_size)
    return shaped.transpose(0, 2, 1, 3).reshape(-1, tile_size * tile_size)


def slot_hits(block_ids, block_counts, block_total):
    slot_count = block_ids.shape[-1]
    live_slot = jnp.arange(slot_count)[None, :] < block_counts[:, None]
    match_block = block_ids[:, :, None] == jnp.arange(block_total)[None, None, :]
    return jnp.where(live_slot[:, :, None] & match_block, 1.0, 0.0).astype(jnp.float32)


def expand_blocks(keep_mask, tile_size, block_rows, block_cols):
    lead_count = keep_mask.shape[0]
    block_grid = keep_mask.reshape(
        lead_count, tile_size // block_rows, 1, tile_size // block_cols, 1
    )
    full_grid = jnp.broadcast_to(
        block_grid,
        (lead_count, tile_size // block_rows, block_rows, tile_size // block_cols, block_cols),
    )
    return full_grid.reshape(lead_count, tile_size, tile_size)


def to_blocks(square_tiles):
    lead_count = square_tiles.shape[0]
    shaped = square_tiles.reshape(lead_count, TILE // BROWS, BROWS, TILE // BCOLS, BCOLS)
    return shaped.transpose(0, 1, 3, 2, 4).reshape(lead_count, BLOCKS, BROWS * BCOLS)


def from_blocks(block_tiles):
    lead_count = block_tiles.shape[0]
    shaped = block_tiles.reshape(lead_count, TILE // BROWS, TILE // BCOLS, BROWS, BCOLS)
    return shaped.transpose(0, 1, 3, 2, 4).reshape(lead_count, TILE, TILE)


def body(hidden_acts, out_grads, momentum, weight_tiles, kept_ids, kept_counts):
    hidden_local = hidden_acts[0]
    grad_out = out_grads[0]
    token_count = hidden_local.shape[0]
    owners = lax.axis_size("shard")
    replicas = lax.axis_size("rep")
    local_count = weight_tiles.shape[0]
    grad_scale = 1.0 / math.sqrt(token_count * owners)
    full_grad = jnp.einsum("tr,td->rd", hidden_local, grad_out, preferred_element_type=jnp.float32)
    summed = lax.psum_scatter(to_tiles(full_grad, TILE), "shard", scatter_dimension=0, tiled=True)
    moment_new = MOMENTUM_DECAY * momentum[0] + grad_scale * summed
    moment_new = moment_new.reshape(local_count, TILE, TILE)
    cos_basis = cosine_basis(TILE)
    coeffs = jnp.einsum("ab,nbc,dc->nad", cos_basis, moment_new, cos_basis, precision=PRECISE)
    hit_table = slot_hits(kept_ids[0], kept_counts[0], BLOCKS)
    keep_mask = jnp.sum(hit_table, axis=1)
    kept_coef = coeffs * expand_blocks(keep_mask, TILE, BROWS, BCOLS)
    moment_out = moment_new - jnp.einsum(
        "ba,nbc,cd->nad", cos_basis, kept_coef, cos_basis, precision=PRECISE
    )
    blocked = to_blocks(kept_coef)
    values = jnp.einsum("jkb,jbv->jkv", hit_table, blocked, precision=PRECISE).astype(jnp.bfloat16)
    piece_vals = lax.all_gather(values[None], "rep", axis=0, tiled=True)
    piece_ids = lax.all_gather(kept_ids, "rep", axis=0, tiled=True)
    one_hot = (piece_ids[..., None] == jnp.arange(BLOCKS)).astype(jnp.bfloat16)
    coef_total = jnp.einsum(
        "rjkb,rjkv->jbv", one_hot, piece_vals, preferred_element_type=jnp.float32
    )
    coef_total = from_blocks(coef_total)
    update = jnp.einsum(
        "ba,nbc,cd->nad", cos_basis, coef_total, cos_basis, precision=PRECISE
    ).reshape(local_count, TILE_SQ)
    new_local = (weight_tiles.astype(jnp.float32) - STEP_FACTOR / replicas * update).astype(
        jnp.bfloat16
    )
    gathered = lax.all_gather(new_local, "shard", axis=0, tiled=True)
    return (gathered, moment_out.reshape(1, local_count, TILE_SQ))


def solution(mesh):
    in_specs = (
        P("rep", "shard", None),
        P("rep", "shard", None),
        P("rep", "shard", None),
        P("shard", None),
        P("rep", "shard", None),
        P("rep", "shard"),
    )
    out_specs = (P(), P("rep", "shard", None))
    return jax.shard_map(body, mesh=mesh, in_specs=in_specs, out_specs=out_specs, check_vma=False)
```

profile of v0, /device:TPU:1, one launch (start us, length us, event | category | flops | bytes accessed | tf_op | source)
XLA Modules:
  0.0 365.9 jit_solution(2266179247445820966)
XLA Ops:
  7.2 3.2 copy.46
  10.5 3.9 %fusion.3 = f32[2,96,64,64]{1,2,3,0:T(8,128)S(1)} fusion(bf16[2,64,256,1]{2,1,3,0:T(8,128)(2,1)S(1)} %bitcast.69, bf16[96,64,256]{2,1,0:T(8,128)(2,1)S(1)} %bitcast.65), kind=kOutput, calls=%fused_computation.3 | convolution fusion | flops 402653184 | bytes 6356992 | tf_op jit(solution)/shard_map/tr,td->rd/dot_general | solution.py:75
  14.4 5.2 %copy.48 = f32[2,96,64,64]{1,0,3,2:T(2,128)} copy(f32[2,96,64,64]{1,2,3,0:T(8,128)S(1)} %fusion.3) | data formatting | bytes 6291456 | tf_op jit(solution)/shard_map/transpose | solution.py:33
  19.6 5.8 %reshape.84 = f32[192,4096]{0,1:T(8,128)} reshape(f32[2,96,64,64]{1,0,3,2:T(2,128)} %copy.48) | data formatting | bytes 6291456 | tf_op jit(solution)/shard_map/reshape | solution.py:33
  25.5 0.7 copy-done.1
  26.2 0.6 copy.44
  27.5 22.6 %all_gather.9 = s32[8,3,4]{2,1,0:T(4,128)S(1)} all-gather(s32[1,3,4]{2,1,0:T(4,128)S(1)} %copy.86), channel_id=1, replica_groups=mesh['shard'=64,'rep'=8] {'rep'}, dimensions={0}, use_global_device_ids=true | all-gather | bytes 432 | tf_op jit(solution)/shard_map/all_gather | solution.py:90
  50.2 1.3 dynamic-slice
  52.1 184.1 %all-reduce.3.cloned.1.call-done = f32[192,4096]{0,1:T(8,128)} async-done(((f32[192,4096]{0,1:T(8,128)}), f32[192,4096]{0,1:T(8,128)}) %all-reduce.3.cloned.1.call-update) | async-done | bytes 3145744
  236.2 4.1 %fusion.6 = f32[3,4096]{0,1:T(8,128)} fusion(f32[192,4096]{0,1:T(8,128)} %all-reduce.3.cloned.1.call-done, u32[]{:T(128)S(6)} %multiply.2, f32[1,3,4096]{1,2,0:T(8,128)S(1)} %copy.44), kind=kLoop, calls=%fused_computation.5 | loop fusion | flops 36864 | bytes 147460 | tf_op jit(solution)/shard_map/add | solution.py:77
  240.3 2.3 copy.61
  242.6 0.4 fusion.15
  243.0 0.4 convolution_multiply_fusion.1
  243.5 0.2 reshape.87
  244.1 20.0 %all-gather = bf16[24,4,128]{2,1,0:T(4,128)(2,1)S(1)} all-gather(bf16[3,4,128]{2,1,0:T(4,128)(2,1)S(1)} %convolution_convert_fusion), channel_id=2, replica_groups=mesh['shard'=64,'rep'=8] {'rep'}, dimensions={0}, use_global_device_ids=true | all-gather | bytes 27648 | tf_op jit(solution)/shard_map/all_gather | solution.py:89
  264.1 0.3 convolution_bitcast_fusion
  264.9 0.5 fusion.12
  265.4 0.4 convolution_multiply_fusion
  265.9 0.6 fusion.7
  266.6 0.5 fusion.9
  267.1 0.4 convolution_subtract_fusion
  267.5 0.7 reshape.99
  268.2 86.6 %all-gather.4.cloned.1.call-done = bf16[64,3,4096]{2,1,0:T(4,128)(2,1)} async-done(((bf16[1,3,4096]{2,1,0:T(4,128)(2,1)}), bf16[64,3,4096]{2,1,0:T(4,128)(2,1)}) %all-gather.4.cloned.1.call-update) | async-done | bytes 1572880 | tf_op jit(solution)/shard_map/all_gather | solution.py:102
  354.8 4.3 %reshape.94 = bf16[192,4096]{1,0:T(8,128)(2,1)} reshape(bf16[64,3,4096]{2,1,0:T(4,128)(2,1)} %all-gather.4.cloned.1.call-done) | data formatting | bytes 3145728
  (30 shorter events, 1.9 us)
Async XLA Ops:
  7.2 3.2 copy-start
  7.2 229.0 %all-reduce.3.cloned.1.call-start = ((), (), s32[]{:S(2)}) async-start(), calls=%async_computation.1 | async-start | bytes 8388608
  25.4 0.8 copy-start.1
  25.4 1.4 copy-start.3
  25.4 1.5 copy-start.4
  25.4 329.4 %all-gather.4.cloned.1.call-start = ((), (), s32[]{:S(2)}) async-start(), calls=%async_computation | async-start | bytes 2129920 | tf_op jit(solution)/shard_map/all_gather | solution.py:102
  240.3 25.6 %copy-start.2 = (bf16[3,4096]{1,0:T(4,128)(2,1)S(1)}, bf16[3,4096]{1,0:T(4,128)(2,1)}, u32[]{:S(2)}) copy-start(bf16[3,4096]{1,0:T(4,128)(2,1)} %param.9) | copy-start | bytes 73732
Sparse Core Ops, SparseCore 0:
  25.6 210.6 all-reduce.2
  266.7 88.0 all-gather.3
where the time goes:
time: 366 us
  waiting for transfers between devices  271 us (74%)
  blocking collectives  42.7 us (12%)
  local copies, waits for them, and re-layouts  25.7 us (7%)
  between operations  14.9 us (4%)
  matrix products  6.95 us (2%)
  other arithmetic  4.92 us (1%)
    unnamed x3, waiting for transfers between devices  184 us
    all_gather x1, waiting for transfers between devices, body(): gathered = lax.all_gather(new_local, 'shard', axis=0, tiled=True)  86.6 us
    all_gather x1, blocking collectives, body(): piece_ids = lax.all_gather(kept_ids, 'rep', axis=0, tiled=True)  22.6 us
    all_gather x1, blocking collectives, body(): piece_vals = lax.all_gather(values[None], 'rep', axis=0, tiled=True)  20 us
    unnamed x16, local copies, waits for them, and re-layouts  10.2 us
  transfers between devices with their start and end apart: 2, of which 2 were waited for; matrix products, arithmetic and copies ran while one was open for 1% of the time, Pallas kernels for 0%

commit v1 on v0

v1 whole, which is shorter than its diff:
```python
import math

import jax
import jax.numpy as jnp
import numpy as np
from jax import lax
from jax.experimental import pallas as pl
from jax.experimental.pallas import tpu as pltpu
from jax.sharding import PartitionSpec as P

TILE = 64
BLOCKS = 32
TILE_SQ = 4096
D = 6144
NX, NY, NZ = 4, 8, 8
ROWS = 96
HALF = 48
PARTS = 4
PART_COLS = D // PARTS
PART_CHIPS = PART_COLS // 384
MOMENTUM_DECAY = 0.9
STEP = 2.0 / 8.0
GRAD_SCALE = 1.0 / 128.0
MESH = pl.DeviceIdType.MESH
F32 = jnp.float32
BF16 = jnp.bfloat16


def constants():
    k = np.arange(TILE, dtype=np.float64)[:, None]
    n = np.arange(TILE, dtype=np.float64)[None, :]
    basis = np.cos(math.pi * (2 * n + 1) * k / (2 * TILE))
    basis *= np.where(k == 0, math.sqrt(1 / TILE), math.sqrt(2 / TILE))
    even, odd = basis[:, 0::2], basis[:, 1::2]
    out = np.zeros((448, 128))
    out[0:128] = np.tile(basis.T, (2, 2))
    out[128:192, 0:64] = basis
    out[192:256, 64:128] = basis
    out[256:384, 0:32] = np.concatenate([even, odd], 0)
    out[384:448, 0:64] = np.concatenate([even.T, odd.T], 0)
    return out.astype(np.float32)


def dot32(a, b):
    return lax.dot_general(
        a, b, (((1,), (0,)), ((), ())), precision=lax.Precision.HIGHEST, preferred_element_type=F32
    )


def iota(shape, dim):
    return lax.broadcasted_iota(jnp.int32, shape, dim)


def kernel(
    hid, grads, mom, wts, ids, counts, consts,
    gath, mom_out,
    gbuf, part, prx, msum, wsum, zbuf, acc, slab,
    s0h, s0f, r0h, r0f, t0h, t0f, u0h, u0f,
    s1h, s1f, r1h, r1f, t1h, t1f, u1h, u1f,
    s2h, s2f, r2h, r2f, t2h, t2f, u2h, u2f,
    load_sem, pair_s, pair_r, rs_s, rs_r, z_s, z_r, ag_s, ag_r, fw_s, fw_r,
):
    shard, z = lax.axis_index("shard"), lax.axis_index("rep")
    c = shard % 2
    y = (shard // 2) % NY
    x = shard // (2 * NY)

    def dev(xx, yy, cc):
        return ((xx * NY + yy) * 2 + cc, z)

    pair = dev(x, y, 1 - c)

    loads = []
    for p in range(PARTS):
        cp = pltpu.make_async_copy(
            grads.at[0, :, pl.ds(p * PART_COLS, PART_COLS)], gbuf.at[p], load_sem.at[p]
        )
        cp.start()
        loads.append(cp)

    barrier = pltpu.get_barrier_semaphore()
    partners = [pair]
    for d in (1, NX - 1):
        partners.append(dev((x + d) % NX, y, c))
    for d in (1, NY - 1):
        partners.append(dev(x, (y + d) % NY, c))
    for d in range(1, NZ):
        partners.append((shard, (z + d) % NZ))
    for who in partners:
        pl.semaphore_signal(barrier, inc=1, device_id=who, device_id_type=MESH)

    r_, c_ = iota((128, 128), 0), iota((128, 128), 1)
    src = (r_ // 64) * 64 + (r_ % 32) * 2 + (r_ % 64) // 32
    perm = jnp.where(c_ == src, 1.0, 0.0).astype(BF16)
    hid_t = lax.dot_general(
        perm, hid[0], (((1,), (1,)), ((), ())), preferred_element_type=F32
    ).astype(BF16)

    for m in range(32):
        msum[pl.ds(m, 3, stride=32), :] = mom[0, :, m * 128:(m + 1) * 128]
        wsum[pl.ds(m, 3, stride=32), :] = wts[:, m * 128:(m + 1) * 128].astype(F32)

    left = iota((32, 128), 1) < 64
    pair_copies = []
    for p in range(PARTS):
        loads[p].wait()
        full = jnp.dot(hid_t, gbuf[p], preferred_element_type=F32)
        for i in range(2):
            for q in range(PART_CHIPS):
                chip = i * 16 + p * PART_CHIPS + q
                for b in range(3):
                    cols = slice(q * 384 + b * 128, q * 384 + (b + 1) * 128)
                    ev = full[i * 64:i * 64 + 32, cols]
                    od = full[i * 64 + 32:i * 64 + 64, cols]
                    first = jnp.where(left, ev, pltpu.roll(od, 64, 1)).astype(BF16)
                    second = jnp.where(left, pltpu.roll(ev, 64, 1), od).astype(BF16)
                    for t, val in ((2 * b, first), (2 * b + 1, second)):
                        row = (t % 3) * 32
                        part[t // 3, chip // 8, chip % 8, row:row + 32, :] = val
        if p == 0:
            pl.semaphore_wait(barrier, len(partners))
        for i in range(2):
            lo = (i * 16 + p * PART_CHIPS) // 8
            yy = (p * PART_CHIPS) % 8
            cp = pltpu.make_async_remote_copy(
                src_ref=part.at[1 - c, lo, pl.ds(yy, PART_CHIPS)],
                dst_ref=prx.at[lo, pl.ds(yy, PART_CHIPS)],
                send_sem=pair_s.at[p * 2 + i],
                recv_sem=pair_r.at[p * 2 + i],
                device_id=pair,
                device_id_type=MESH,
            )
            cp.start()
            pair_copies.append(cp)
    for cp in pair_copies:
        cp.wait()

    def ring_reduce(n, pos, who, local, bufs, base):
        sh, sf, rh, rf, th, tf, uh, uf = bufs
        h = n // 2
        copies = []
        prev = None
        for t in range(h):
            o = h - t
            right, lft = (pos + o) % n, (pos + n - o) % n
            if t == 0:
                sh[...] = local(right, 0, HALF).astype(BF16)
                th[...] = local(lft, HALF, ROWS).astype(BF16)
                pairs = ((sh, rh), (th, uh))
            else:
                a, b = sf.at[t - 1], tf.at[t - 1]
                if t == 1:
                    a[..., 0:HALF, :] = (local(right, 0, HALF) + rh[...].astype(F32)).astype(BF16)
                    a[..., HALF:ROWS, :] = local(right, HALF, ROWS).astype(BF16)
                    b[..., 0:HALF, :] = local(lft, 0, HALF).astype(BF16)
                    b[..., HALF:ROWS, :] = (local(lft, HALF, ROWS) + uh[...].astype(F32)).astype(BF16)
                else:
                    a[...] = (local(right, 0, ROWS) + rf[t - 2].astype(F32)).astype(BF16)
                    b[...] = (local(lft, 0, ROWS) + uf[t - 2].astype(F32)).astype(BF16)
                pairs = ((a, rf.at[t - 1]), (b, uf.at[t - 1]))
            now = []
            for k, (s, r) in enumerate(pairs):
                cp = pltpu.make_async_remote_copy(
                    src_ref=s, dst_ref=r,
                    send_sem=rs_s.at[base + 2 * t + k], recv_sem=rs_r.at[base + 2 * t + k],
                    device_id=who((pos + (1 if k == 0 else n - 1)) % n), device_id_type=MESH,
                )
                cp.start()
                now.append(cp)
            for cp in now:
                cp.wait_recv()
            copies += now
        total = local(pos, 0, ROWS) + rf[h - 2].astype(F32) + uf[h - 2].astype(F32)
        for cp in copies:
            cp.wait_send()
        return total

    def own(ix):
        return part[(c,) + ix].astype(F32) + prx[ix].astype(F32)

    y_of = lambda v: dev(x, v, c)
    x_of = lambda v: dev(v, y, c)
    bufs0 = (s0h, s0f, r0h, r0f, t0h, t0f, u0h, u0f)
    bufs1 = (s1h, s1f, r1h, r1f, t1h, t1f, u1h, u1f)

    bufs2 = (s2h, s2f, r2h, r2f, t2h, t2f, u2h, u2f)

    def summed(v, lo, hi):
        return acc[v, lo:hi]

    @pl.when(c == 0)
    def _():
        acc[0:NX] = ring_reduce(
            NY, y, y_of, lambda v, lo, hi: own((slice(None), v, slice(lo, hi))), bufs0, 0
        )
        slab[...] = ring_reduce(NX, x, x_of, summed, bufs2, 8)

    @pl.when(c == 1)
    def _():
        acc[...] = ring_reduce(
            NX, x, x_of, lambda v, lo, hi: own((v, slice(None), slice(lo, hi))), bufs1, 0
        )
        slab[...] = ring_reduce(NY, y, y_of, summed, bufs2, 4)

    moment = MOMENTUM_DECAY * msum[...] + GRAD_SCALE * slab[...]
    both, diag = consts[0:128], consts[128:256]
    fwd, inv = consts[256:384, 0:32], consts[384:448, 0:64]
    tiles = jnp.concatenate([moment[0:32], moment[32:64], moment[64:96]], axis=1)
    v = dot32(fwd, tiles)
    left64 = iota((64, 128), 1) < 64
    v = jnp.concatenate(
        [
            jnp.where(left64, v[0:64, k * 128:(k + 1) * 128], v[64:128, k * 128:(k + 1) * 128])
            for k in range(3)
        ],
        axis=0,
    )
    coef = dot32(v, both)

    group = (iota((64, 128), 1) % 64) // 16
    unit = (iota((64, 128), 0) // 8) * 4 + group
    kept = []
    for k in range(3):
        keep = jnp.zeros((64, 128), F32)
        for j in range(4):
            live = jnp.where(j < counts[0, k], ids[0, k, j], -1)
            keep = jnp.where(unit == live, 1.0, keep)
        kept.append(coef[k * 64:(k + 1) * 64] * keep)

    lane8 = iota((8, 128), 1)
    row8 = iota((8, 128), 0)
    picked = []
    numbers = jnp.zeros((8, 128), F32)
    for k in range(3):
        for j in range(4):
            number = ids[0, k, j]
            block = jnp.zeros((8, 128), F32)
            for p in range(8):
                block = jnp.where(number // 4 == p, kept[k][p * 8:(p + 1) * 8], block)
            here = (lane8 // 16) == number % 4
            picked.append(jnp.where(here & (j < counts[0, k]), block, 0.0))
            slot = (row8 == k) & (lane8 // 16 == 4 + j)
            numbers = jnp.where(slot, number.astype(F32), numbers)
    picked = jnp.concatenate(picked, axis=0).astype(BF16)
    spread = jnp.where(
        iota((128, 128), 0) % 16 == iota((128, 128), 1) % 16, 1.0, 0.0
    ).astype(BF16)
    picked = jnp.dot(picked, spread, preferred_element_type=F32)
    halves = [jnp.zeros((8, 128), F32), numbers]
    for k in range(3):
        for j in range(4):
            at = (k * 4 + j) * 8
            halves[k // 2] = jnp.where(
                lane8 // 16 == (k % 2) * 4 + j, picked[at:at + 8], halves[k // 2]
            )
    zbuf[z] = jnp.concatenate(halves, axis=0).astype(BF16)
    sends = []
    for d in range(1, NZ):
        cp = pltpu.make_async_remote_copy(
            src_ref=zbuf.at[z], dst_ref=zbuf.at[z],
            send_sem=z_s.at[d - 1], recv_sem=z_r.at[d - 1],
            device_id=(shard, (z + d) % NZ), device_id_type=MESH,
        )
        cp.start()
        sends.append(cp)

    def inverse(rows):
        kb = dot32(rows, diag)
        kb = jnp.concatenate([kb[0:64], kb[64:128], kb[128:192]], axis=1)
        w = dot32(inv, kb)
        return jnp.concatenate(
            [
                jnp.where(left, w[0:32, k * 128:(k + 1) * 128], w[32:64, k * 128:(k + 1) * 128])
                for k in range(3)
            ],
            axis=0,
        )

    msum[...] = moment - inverse(jnp.concatenate(kept, axis=0))
    for m in range(32):
        mom_out[0, :, m * 128:(m + 1) * 128] = msum[pl.ds(m, 3, stride=32), :]

    for d in range(1, NZ):
        frm = (z + NZ - d) % NZ
        pltpu.make_async_remote_copy(
            src_ref=zbuf.at[z], dst_ref=zbuf.at[frm],
            send_sem=z_s.at[d - 1], recv_sem=z_r.at[d - 1],
            device_id=(shard, frm), device_id_type=MESH,
        ).wait_recv()

    wide = iota((128, 1024), 1)
    pick = (wide // 128 == iota((128, 1024), 0) // 16) & (wide % 16 == iota((128, 1024), 0) % 16)
    pick = jnp.where(pick, 1.0, 0.0).astype(BF16)
    msgs = jnp.concatenate([zbuf[r] for r in range(NZ)], axis=0)
    vals = jnp.dot(msgs, pick, preferred_element_type=F32)
    unitf = unit.astype(F32)
    totals = []
    for k in range(3):
        total = jnp.zeros((64, 128), F32)
        for r in range(NZ):
            for j in range(4):
                col = ((k % 2) * 4 + j) * 128
                row = r * 16 + (k // 2) * 8
                val = vals[row:row + 8, col:col + 128]
                num = vals[r * 16 + 8 + k:r * 16 + 9 + k, (4 + j) * 128:(5 + j) * 128]
                val = jnp.concatenate([val] * 8, axis=0)
                total = total + jnp.where(unitf == num, val, 0.0)
        totals.append(total)
    update = inverse(jnp.concatenate(totals, axis=0))
    gath[x, y, c] = (wsum[...] - STEP * update).astype(BF16)

    def hand_on(chunk, k):
        return pltpu.make_async_remote_copy(
            src_ref=chunk, dst_ref=chunk, send_sem=fw_s.at[k], recv_sem=fw_r.at[k],
            device_id=pair, device_id_type=MESH,
        )

    def ring_gather(n, pos, who, chunk, base, arrived):
        h = n // 2
        copies = []
        for t in range(1, h + 1):
            lo, hi = ((0, HALF), (HALF, ROWS)) if t == h else ((0, ROWS), (0, ROWS))
            now = []
            for k, (at, to, rows) in enumerate((
                ((pos + n - (t - 1)) % n, (pos + 1) % n, lo), ((pos + t - 1) % n, (pos + n - 1) % n, hi)
            )):
                ref = chunk(at, *rows)
                cp = pltpu.make_async_remote_copy(
                    src_ref=ref, dst_ref=ref,
                    send_sem=ag_s.at[base + 2 * (t - 1) + k], recv_sem=ag_r.at[base + 2 * (t - 1) + k],
                    device_id=who(to), device_id_type=MESH,
                )
                cp.start()
                now.append(cp)
            for k, (cp, at, rows) in enumerate(
                zip(now, ((pos + n - t) % n, (pos + t) % n), (lo, hi))
            ):
                ref = chunk(at, *rows)
                pltpu.make_async_remote_copy(
                    src_ref=ref, dst_ref=ref,
                    send_sem=ag_s.at[base + 2 * (t - 1) + k], recv_sem=ag_r.at[base + 2 * (t - 1) + k],
                    device_id=pair, device_id_type=MESH,
                ).wait_recv()
                if arrived is not None:
                    arrived(at, rows, 2 * (t - 1) + k + 1)
            copies += now
        for cp in copies:
            cp.wait_send()

    def column(cc):
        return lambda v, lo=0, hi=ROWS: gath.at[:, v, cc, pl.ds(lo, hi - lo)]

    def line(cc):
        return lambda v, lo=0, hi=ROWS: gath.at[v, :, cc, pl.ds(lo, hi - lo)]

    def one_x(v, lo, hi):
        return gath.at[v, y, c, pl.ds(lo, hi - lo)]

    def one_y(v, lo, hi):
        return gath.at[x, v, c, pl.ds(lo, hi - lo)]

    def passed_on(n, pos, chunk):
        out = [hand_on(chunk(pos), 0)]
        for t in range(1, n // 2 + 1):
            lo, hi = ((0, HALF), (HALF, ROWS)) if t == n // 2 else ((0, ROWS), (0, ROWS))
            out.append(hand_on(chunk((pos + n - t) % n, *lo), 2 * t - 1))
            out.append(hand_on(chunk((pos + t) % n, *hi), 2 * t))
        return out

    def finish(n, pos, who, chunk, base, other_n, other_pos, other_chunk):
        mine = passed_on(n, pos, chunk)
        mine[0].start()
        ring_gather(n, pos, who, chunk, base, lambda at, rows, k: mine[k].start())
        for cp in passed_on(other_n, other_pos, other_chunk):
            cp.wait_recv()
        for cp in mine:
            cp.wait_send()

    @pl.when(c == 0)
    def _():
        ring_gather(NX, x, x_of, one_x, 8, None)
        finish(NY, y, y_of, column(0), 0, NX, x, line(1))

    @pl.when(c == 1)
    def _():
        ring_gather(NY, y, y_of, one_y, 4, None)
        finish(NX, x, x_of, line(1), 0, NY, y, column(0))

    for cp in sends:
        cp.wait_send()


def body(hidden_acts, out_grads, momentum, weight_tiles, kept_ids, kept_counts):
    vmem = pl.BlockSpec(memory_space=pltpu.VMEM)
    smem = pl.BlockSpec(memory_space=pltpu.SMEM)

    def ring_bufs(lead, steps):
        half = pltpu.VMEM(lead + (HALF, 128), BF16)
        whole = pltpu.VMEM((steps,) + lead + (ROWS, 128), BF16)
        return [half, whole] * 4

    dma = pltpu.SemaphoreType.DMA
    gathered, moment_out = pl.pallas_call(
        kernel,
        out_shape=(
            jax.ShapeDtypeStruct((NX, NY, 2, ROWS, 128), BF16),
            jax.ShapeDtypeStruct((1, 3, TILE_SQ), F32),
        ),
        in_specs=[vmem, pl.BlockSpec(memory_space=pl.ANY), vmem, vmem, smem, smem, vmem],
        out_specs=(vmem, vmem),
        scratch_shapes=[
            pltpu.VMEM((PARTS, 256, PART_COLS), BF16),
            pltpu.VMEM((2, NX, NY, ROWS, 128), BF16),
            pltpu.VMEM((NX, NY, ROWS, 128), BF16),
            pltpu.VMEM((ROWS, 128), F32),
            pltpu.VMEM((ROWS, 128), F32),
            pltpu.VMEM((NZ, 16, 128), BF16),
            pltpu.VMEM((NY, ROWS, 128), F32),
            pltpu.VMEM((ROWS, 128), F32),
            *ring_bufs((NX,), 3),
            *ring_bufs((NY,), 1),
            *ring_bufs((), 3),
            dma((PARTS,)),
            dma((2 * PARTS,)),
            dma((2 * PARTS,)),
            dma((12,)),
            dma((12,)),
            dma((NZ - 1,)),
            dma((NZ - 1,)),
            dma((12,)),
            dma((12,)),
            dma((9,)),
            dma((9,)),
        ],
        compiler_params=pltpu.CompilerParams(
            collective_id=0, has_side_effects=True, vmem_limit_bytes=48 * 1024 * 1024
        ),
    )(
        hidden_acts, out_grads, momentum, weight_tiles, kept_ids, kept_counts, jnp.asarray(constants())
    )
    return gathered.reshape(192, TILE_SQ), moment_out


def solution(mesh):
    in_specs = (
        P("rep", "shard", None),
        P("rep", "shard", None),
        P("rep", "shard", None),
        P("shard", None),
        P("rep", "shard", None),
        P("rep", "shard"),
    )
    out_specs = (P(), P("rep", "shard", None))
    return jax.shard_map(body, mesh=mesh, in_specs=in_specs, out_specs=out_specs, check_vma=False)
```

time: 366 us -> 81.9 us (0.22)
  waiting for transfers between devices: 271 us -> 0 us
  Pallas kernels: 0 us -> 71.6 us
  blocking collectives: 42.7 us -> 0 us
  local copies, waits for them, and re-layouts: 25.7 us -> 9.32 us
  between operations: 14.9 us -> 0.65 us
  matrix products: 6.95 us -> 0 us
  other arithmetic: 4.92 us -> 0 us
    unnamed x3 -> x0, waiting for transfers between devices: 184 us -> none
    all_gather x1 -> x0, waiting for transfers between devices: 86.6 us -> none  [body(): gathered = lax.all_gather(new_local, 'shard', axis=0, tiled=True)]
    pallas_call x0 -> x1, Pallas kernels: none -> 71.6 us  [body(): pl.pallas_call(kernel, out_shape=(jax.ShapeDtypeStruct((NX, NY, 2, ROWS,...]
    all_gather x2 -> x0, blocking collectives: 42.7 us -> none  [the longest x1 22.6 us: body(): piece_ids = lax.all_gather(kept_ids, 'rep', axis=0, tiled=True)]
    reshape x9 -> x1, local copies, waits for them, and re-layouts: 9.89 us -> 2.06 us  [body(): return (gathered.reshape(192, TILE_SQ), moment_out)]
    dot_general x9 -> x0, matrix products: 6.95 us -> none  [the longest x1 3.85 us: body(): jnp.einsum('tr,td->rd', hidden_local, grad_out, preferred_element_type=jn...]
    transpose x2 -> x0, local copies, waits for them, and re-layouts: 5.21 us -> none  [the longest x1 5.18 us: to_tiles(): return shaped.transpose(0, 2, 1, 3).reshape(-1, tile_size * tile_size)]
    add x1 -> x0, other arithmetic: 4.11 us -> none  [body(): moment_new = MOMENTUM_DECAY * momentum[0] + grad_scale * summed]
  transfers between devices with their start and end apart: 2 -> 0, of which waited for: 2 -> 0; matrix products, arithmetic and copies ran while one was open for 1% -> 0% of each run, Pallas kernels for 0% -> 0%
where the time goes in v1:
time: 81.9 us; the launch traced here: 81.5 us
  Pallas kernels  71.6 us (87%)
  local copies, waits for them, and re-layouts  9.32 us (11%)
    pallas_call x1, Pallas kernels, body(): pl.pallas_call(kernel, out_shape=(jax.ShapeDtypeStruct((NX, NY, 2, ROWS,...  71.6 us
    unnamed x13, local copies, waits for them, and re-layouts  7.26 us
    reshape x1, local copies, waits for them, and re-layouts, body(): return (gathered.reshape(192, TILE_SQ), moment_out)  2.06 us

profile of v1, /device:TPU:1, one launch (start us, length us, event | category | flops | bytes accessed | tf_op | source)
XLA Modules:
  0.0 81.5 jit_solution(1702608221784477858)
XLA Ops:
  0.6 0.7 copy.10.ids
  1.3 0.8 %copy.9.mom = f32[1,3,4096]{2,1,0:T(4,128)S(1)} copy(f32[1,3,4096]{2,0,1:T(1,128)} %param.9) | data formatting | bytes 98304 | tf_op args[2]
  2.1 0.0 copy-start
  2.2 1.9 %copy-done = bf16[1,256,6144]{2,1,0:T(8,128)(2,1)S(1)} copy-done((bf16[1,256,6144]{2,1,0:T(8,128)(2,1)S(1)}, bf16[1,256,6144]{2,1,0:T(8,128)(2,1)}, u32[]{:S(2)}) %copy-start) | copy-done | bytes 3145752
  4.0 0.0 copy-start.1
  4.0 0.9 %copy-done.1 = f32[448,128]{1,0:T(8,128)S(1)} copy-done((f32[448,128]{1,0:T(8,128)S(1)}, f32[448,128]{1,0:T(8,128)}, u32[]{:S(2)}) %copy-start.1) | copy-done | bytes 229400
  5.0 0.0 copy-start.2
  5.0 0.8 %copy-done.2 = bf16[1,256,128]{2,1,0:T(8,128)(2,1)S(1)} copy-done((bf16[1,256,128]{2,1,0:T(8,128)(2,1)S(1)}, bf16[1,256,128]{2,1,0:T(8,128)(2,1)}, u32[]{:S(2)}) %copy-start.2) | copy-done | bytes 65560
  5.8 0.0 copy-start.3
  5.8 0.8 copy-done.3
  6.6 0.0 copy-start.4
  6.6 0.7 copy-done.4
  7.2 71.6 %shard_map.86 = (bf16[4,8,2,96,128]{4,3,2,1,0:T(8,128)(2,1)S(1)}, f32[1,3,4096]{2,1,0:T(4,128)S(1)}) custom-call(bf16[1,256,128]{2,1,0:T(8,128)(2,1)S(1)} %copy-done.2, bf16[1,256,6144]{2,1,0:T(8,128)(2,1)S(1)} %copy-done, f32[1,3,4096]{2,1,0:T(4,128)S(1)} %copy.9.mom, bf16[3,4096]{1,0:T(4,128)(2,1)S(1)} %copy-done.3, s32[1,3,4]{2,1,0:T(4,128)S(1)} %copy.10.ids, ...), custom_call_target="tpu_custom_call" | custom-call | tf_op jit(solution)/shard_map/pallas_call | solution.py:403
  78.8 2.1 %reshape.7 = bf16[192,4096]{1,0:T(8,128)(2,1)} reshape(bf16[4,8,2,96,128]{4,3,2,1,0:T(8,128)(2,1)S(1)} %get-tuple-element.4) | data formatting | bytes 3145728 | tf_op jit(solution)/shard_map/reshape | solution.py:441
  80.9 0.7 copy.11
Async XLA Ops:
  2.1 1.9 %copy-start = (bf16[1,256,6144]{2,1,0:T(8,128)(2,1)S(1)}, bf16[1,256,6144]{2,1,0:T(8,128)(2,1)}, u32[]{:S(2)}) copy-start(bf16[1,256,6144]{2,1,0:T(8,128)(2,1)} %grads.1) | copy-start | bytes 9437188
  4.0 0.9 %copy-start.1 = (f32[448,128]{1,0:T(8,128)S(1)}, f32[448,128]{1,0:T(8,128)}, u32[]{:S(2)}) copy-start(f32[448,128]{1,0:T(8,128)} %constant.2.clone.consts) | copy-start | bytes 688132
  5.0 0.8 %copy-start.2 = (bf16[1,256,128]{2,1,0:T(8,128)(2,1)S(1)}, bf16[1,256,128]{2,1,0:T(8,128)(2,1)}, u32[]{:S(2)}) copy-start(bf16[1,256,128]{2,1,0:T(8,128)(2,1)} %hid.1) | copy-start | bytes 196612
  5.8 0.8 copy-start.3
  6.6 0.7 copy-start.4

commit v2 on v1

v2 whole, which is shorter than its diff:
```python
import math

import jax
import jax.numpy as jnp
import numpy as np
from jax import lax
from jax.experimental import pallas as pl
from jax.experimental.pallas import tpu as pltpu
from jax.sharding import PartitionSpec as P

TILE = 64
BLOCKS = 32
TILE_SQ = 4096
D = 6144
NX, NY, NZ = 4, 8, 8
ROWS = 96
Y_ROWS = 32
G_ROWS = 32
X_NEAR = (1, 3, 2)
Y_NEAR = (1, 7, 2, 6, 3, 5, 4)
PARTS = 4
PART_COLS = D // PARTS
PART_CHIPS = PART_COLS // 384
BARRIER_AT = 3
MOMENTUM_DECAY = 0.9
STEP = 2.0 / 8.0
GRAD_SCALE = 1.0 / 128.0
MESH = pl.DeviceIdType.MESH
F32 = jnp.float32
BF16 = jnp.bfloat16


def constants():
    k = np.arange(TILE, dtype=np.float64)[:, None]
    n = np.arange(TILE, dtype=np.float64)[None, :]
    basis = np.cos(math.pi * (2 * n + 1) * k / (2 * TILE))
    basis *= np.where(k == 0, math.sqrt(1 / TILE), math.sqrt(2 / TILE))
    even, odd = basis[:, 0::2], basis[:, 1::2]
    out = np.zeros((448, 128))
    out[0:128] = np.tile(basis.T, (2, 2))
    out[128:192, 0:64] = basis
    out[192:256, 64:128] = basis
    out[256:384, 0:32] = np.concatenate([even, odd], 0)
    out[384:448, 0:64] = np.concatenate([even.T, odd.T], 0)
    return out.astype(np.float32)


def dot32(a, b):
    return lax.dot_general(
        a, b, (((1,), (0,)), ((), ())), precision=lax.Precision.HIGHEST, preferred_element_type=F32
    )


def iota(shape, dim):
    return lax.broadcasted_iota(jnp.int32, shape, dim)


def kernel(
    hid, grads, mom, wts, ids, counts, consts,
    gath, mom_out,
    hid_v, gbuf, mom_v, wts_v, ids_v, counts_v, consts_v,
    part, prx, wsum, zbuf, slab, acc_y, acc_x,
    st_y1, rx_y1, st_x1, rx_x1, st_y2, rx_y2, st_x2, rx_x2,
    load_sem, in_sem, pair_s, pair_r,
    y1_s, y1_r, x1_s, x1_r, y2_s, y2_r, x2_s, x2_r,
    z_s, z_r, gy_s, gy_r, gx_s, gx_r, ry_s, ry_r, rx_s, rx_r, fw_s, fw_r,
):
    shard, z = lax.axis_index("shard"), lax.axis_index("rep")
    c = shard % 2
    y = (shard // 2) % NY
    x = shard // (2 * NY)

    def dev(xx, yy, cc):
        return ((xx * NY + yy) * 2 + cc, z)

    def y_at(d):
        return (y + d) % NY

    def x_at(d):
        return (x + d) % NX

    def to_y(d):
        return dev(x, y_at(d), c)

    def to_x(d):
        return dev(x_at(d), y, c)

    def remote(src, dst, send, recv, who):
        return pltpu.make_async_remote_copy(
            src_ref=src, dst_ref=dst, send_sem=send, recv_sem=recv,
            device_id=who, device_id_type=MESH,
        )

    pair = dev(x, y, 1 - c)
    barrier = pltpu.get_barrier_semaphore()
    partners = [pair] + [to_x(d) for d in X_NEAR] + [to_y(d) for d in Y_NEAR]
    partners += [(shard, (z + d) % NZ) for d in range(1, NZ)]
    for who in partners:
        pl.semaphore_signal(barrier, inc=1, device_id=who, device_id_type=MESH)

    moves = []
    for k, (src, dst) in enumerate((
        (hid.at[0], hid_v), (mom, mom_v), (wts, wts_v), (ids, ids_v), (counts, counts_v),
        (consts, consts_v),
    )):
        moves.append(pltpu.make_async_copy(src, dst, in_sem.at[k]))
    moves[0].start()
    loads = []
    for p in range(PARTS):
        cp = pltpu.make_async_copy(
            grads.at[0, :, pl.ds(p * PART_COLS, PART_COLS)], gbuf.at[p], load_sem.at[p]
        )
        cp.start()
        loads.append(cp)
    for cp in moves[1:]:
        cp.start()
    moves[0].wait()

    r_, c_ = iota((128, 128), 0), iota((128, 128), 1)
    src = (r_ // 64) * 64 + (r_ % 32) * 2 + (r_ % 64) // 32
    perm = jnp.where(c_ == src, 1.0, 0.0).astype(BF16)
    hid_t = lax.dot_general(
        perm, hid_v[...], (((1,), (1,)), ((), ())), preferred_element_type=F32
    ).astype(BF16)

    left = iota((32, 128), 1) < 64
    pair_copies = []
    for p in range(PARTS):
        loads[p].wait()
        full = jnp.dot(hid_t, gbuf[p], preferred_element_type=F32)
        for i in range(2):
            for q in range(PART_CHIPS):
                chip = i * 16 + p * PART_CHIPS + q
                for b in range(3):
                    cols = slice(q * 384 + b * 128, q * 384 + (b + 1) * 128)
                    ev = full[i * 64:i * 64 + 32, cols]
                    od = full[i * 64 + 32:i * 64 + 64, cols]
                    first = jnp.where(left, ev, pltpu.roll(od, 64, 1)).astype(BF16)
                    second = jnp.where(left, pltpu.roll(ev, 64, 1), od).astype(BF16)
                    for t, val in ((2 * b, first), (2 * b + 1, second)):
                        row = (t % 3) * 32
                        part[t // 3, chip // 8, chip % 8, row:row + 32, :] = val
        if p == BARRIER_AT:
            pl.semaphore_wait(barrier, len(partners))
        for i in range(2):
            lo = (i * 16 + p * PART_CHIPS) // 8
            yy = (p * PART_CHIPS) % 8
            cp = pltpu.make_async_remote_copy(
                src_ref=part.at[1 - c, lo, pl.ds(yy, PART_CHIPS)],
                dst_ref=prx.at[lo, pl.ds(yy, PART_CHIPS)],
                send_sem=pair_s.at[p * 2 + i],
                recv_sem=pair_r.at[p * 2 + i],
                device_id=pair,
                device_id_type=MESH,
            )
            pair_copies.append(cp)
        if p >= BARRIER_AT:
            for cp in pair_copies[0 if p == BARRIER_AT else -2:]:
                cp.start()
    for cp in pair_copies:
        cp.wait()


    def own(ix):
        return part[(c,) + ix].astype(F32) + prx[ix].astype(F32)

    ys, xs = slice(0, Y_ROWS), slice(Y_ROWS, ROWS)
    every = slice(None)
    first_x, first_y, second_y, second_x = [], [], [], []
    for d in X_NEAR:
        st_x1[d - 1] = own((x_at(d), every, xs)).astype(BF16)
        cp = remote(st_x1.at[d - 1], rx_x1.at[d - 1], x1_s.at[d - 1], x1_r.at[d - 1], to_x(d))
        cp.start()
        first_x.append(cp)
    for d in Y_NEAR:
        st_y1[d - 1] = own((every, y_at(d), ys)).astype(BF16)
        cp = remote(st_y1.at[d - 1], rx_y1.at[d - 1], y1_s.at[d - 1], y1_r.at[d - 1], to_y(d))
        cp.start()
        first_y.append(cp)
    total = own((x, every, xs))
    for cp, d in zip(first_x, X_NEAR):
        cp.wait_recv()
        total = total + rx_x1[d - 1].astype(F32)
    acc_x[...] = total
    for d in Y_NEAR:
        st_y2[d - 1] = acc_x[y_at(d)].astype(BF16)
        cp = remote(st_y2.at[d - 1], rx_y2.at[d - 1], y2_s.at[d - 1], y2_r.at[d - 1], to_y(d))
        cp.start()
        second_y.append(cp)
    total = own((every, y, ys))
    for cp, d in zip(first_y, Y_NEAR):
        cp.wait_recv()
        total = total + rx_y1[d - 1].astype(F32)
    acc_y[...] = total
    for d in X_NEAR:
        st_x2[d - 1] = acc_y[x_at(d)].astype(BF16)
        cp = remote(st_x2.at[d - 1], rx_x2.at[d - 1], x2_s.at[d - 1], x2_r.at[d - 1], to_x(d))
        cp.start()
        second_x.append(cp)
    total = acc_x[y]
    for cp, d in zip(second_y, Y_NEAR):
        cp.wait_recv()
        total = total + rx_y2[d - 1].astype(F32)
    slab[xs] = total
    total = acc_y[x]
    for cp, d in zip(second_x, X_NEAR):
        cp.wait_recv()
        total = total + rx_x2[d - 1].astype(F32)
    slab[ys] = total
    for cp in moves[1:]:
        cp.wait()

    moment = MOMENTUM_DECAY * mom_v[...] + GRAD_SCALE * slab[...]
    both, diag = consts_v[0:128], consts_v[128:256]
    fwd, inv = consts_v[256:384, 0:32], consts_v[384:448, 0:64]
    tiles = jnp.concatenate([moment[0:32], moment[32:64], moment[64:96]], axis=1)
    v = dot32(fwd, tiles)
    left64 = iota((64, 128), 1) < 64
    v = jnp.concatenate(
        [
            jnp.where(left64, v[0:64, k * 128:(k + 1) * 128], v[64:128, k * 128:(k + 1) * 128])
            for k in range(3)
        ],
        axis=0,
    )
    coef = dot32(v, both)

    group = (iota((64, 128), 1) % 64) // 16
    unit = (iota((64, 128), 0) // 8) * 4 + group
    kept = []
    for k in range(3):
        keep = jnp.zeros((64, 128), F32)
        for j in range(4):
            live = jnp.where(j < counts_v[0, k], ids_v[k, 0, j], -1)
            keep = jnp.where(unit == live, 1.0, keep)
        kept.append(coef[k * 64:(k + 1) * 64] * keep)

    lane8 = iota((8, 128), 1)
    row8 = iota((8, 128), 0)
    picked = []
    numbers = jnp.zeros((8, 128), F32)
    for k in range(3):
        for j in range(4):
            number = ids_v[k, 0, j]
            block = jnp.zeros((8, 128), F32)
            for p in range(8):
                block = jnp.where(number // 4 == p, kept[k][p * 8:(p + 1) * 8], block)
            here = (lane8 // 16) == number % 4
            picked.append(jnp.where(here & (j < counts_v[0, k]), block, 0.0))
            slot = (row8 == k) & (lane8 // 16 == 4 + j)
            numbers = jnp.where(slot, number.astype(F32), numbers)
    picked = jnp.concatenate(picked, axis=0).astype(BF16)
    spread = jnp.where(
        iota((128, 128), 0) % 16 == iota((128, 128), 1) % 16, 1.0, 0.0
    ).astype(BF16)
    picked = jnp.dot(picked, spread, preferred_element_type=F32)
    halves = [jnp.zeros((8, 128), F32), numbers]
    for k in range(3):
        for j in range(4):
            at = (k * 4 + j) * 8
            halves[k // 2] = jnp.where(
                lane8 // 16 == (k % 2) * 4 + j, picked[at:at + 8], halves[k // 2]
            )
    zbuf[z] = jnp.concatenate(halves, axis=0).astype(BF16)
    sends = []
    for d in range(1, NZ):
        cp = pltpu.make_async_remote_copy(
            src_ref=zbuf.at[z], dst_ref=zbuf.at[z],
            send_sem=z_s.at[d - 1], recv_sem=z_r.at[d - 1],
            device_id=(shard, (z + d) % NZ), device_id_type=MESH,
        )
        cp.start()
        sends.append(cp)

    def inverse(rows):
        kb = dot32(rows, diag)
        kb = jnp.concatenate([kb[0:64], kb[64:128], kb[128:192]], axis=1)
        w = dot32(inv, kb)
        return jnp.concatenate(
            [
                jnp.where(left, w[0:32, k * 128:(k + 1) * 128], w[32:64, k * 128:(k + 1) * 128])
                for k in range(3)
            ],
            axis=0,
        )

    mom_out[...] = moment - inverse(jnp.concatenate(kept, axis=0))
    for m in range(32):
        wsum[pl.ds(m, 3, stride=32), :] = wts_v[:, m * 128:(m + 1) * 128].astype(F32)

    for d in range(1, NZ):
        frm = (z + NZ - d) % NZ
        pltpu.make_async_remote_copy(
            src_ref=zbuf.at[z], dst_ref=zbuf.at[frm],
            send_sem=z_s.at[d - 1], recv_sem=z_r.at[d - 1],
            device_id=(shard, frm), device_id_type=MESH,
        ).wait_recv()

    wide = iota((128, 1024), 1)
    pick = (wide // 128 == iota((128, 1024), 0) // 16) & (wide % 16 == iota((128, 1024), 0) % 16)
    pick = jnp.where(pick, 1.0, 0.0).astype(BF16)
    msgs = jnp.concatenate([zbuf[r] for r in range(NZ)], axis=0)
    vals = jnp.dot(msgs, pick, preferred_element_type=F32)
    unitf = unit.astype(F32)
    totals = []
    for k in range(3):
        total = jnp.zeros((64, 128), F32)
        for r in range(NZ):
            for j in range(4):
                col = ((k % 2) * 4 + j) * 128
                row = r * 16 + (k // 2) * 8
                val = vals[row:row + 8, col:col + 128]
                num = vals[r * 16 + 8 + k:r * 16 + 9 + k, (4 + j) * 128:(5 + j) * 128]
                val = jnp.concatenate([val] * 8, axis=0)
                total = total + jnp.where(unitf == num, val, 0.0)
        totals.append(total)
    update = inverse(jnp.concatenate(totals, axis=0))
    gath[x, y, c] = (wsum[...] - STEP * update).astype(BF16)


    sends += first_x + first_y + second_x + second_y
    lower, upper = pl.ds(0, G_ROWS), pl.ds(G_ROWS, ROWS - G_ROWS)

    def same(ref, send, recv, who):
        return remote(ref, ref, send, recv, who)

    mine = gath.at[x, y, c]
    for d in X_NEAR:
        cp = same(mine, gx_s.at[d - 1], gx_r.at[d - 1], to_x(d))
        cp.start()
        sends.append(cp)
    for d in Y_NEAR:
        cp = same(mine, gy_s.at[d - 1], gy_r.at[d - 1], to_y(d))
        cp.start()
        sends.append(cp)

    def hand_on(cc, dx, dy):
        k = dx * NY + dy
        return same(gath.at[x_at(NX - dx), y_at(NY - dy), cc], fw_s.at[k], fw_r.at[k], pair)

    def give(dx, dy):
        cp = hand_on(c, dx, dy)
        cp.start()
        sends.append(cp)

    give(0, 0)
    for dx in X_NEAR:
        src = gath.at[x_at(NX - dx), y, c]
        same(src, gx_s.at[dx - 1], gx_r.at[dx - 1], pair).wait_recv()
        for dy in Y_NEAR:
            k = (dx - 1) * 7 + dy - 1
            cp = same(src.at[lower], ry_s.at[k], ry_r.at[k], to_y(dy))
            cp.start()
            sends.append(cp)
        give(dx, 0)
    for dy in Y_NEAR:
        src = gath.at[x, y_at(NY - dy), c]
        same(src, gy_s.at[dy - 1], gy_r.at[dy - 1], pair).wait_recv()
        for dx in X_NEAR:
            k = (dx - 1) * 7 + dy - 1
            cp = same(src.at[upper], rx_s.at[k], rx_r.at[k], to_x(dx))
            cp.start()
            sends.append(cp)
        give(0, dy)
    for dy in Y_NEAR:
        for dx in X_NEAR:
            k = (dx - 1) * 7 + dy - 1
            dst = gath.at[x_at(NX - dx), y_at(NY - dy), c]
            same(dst.at[lower], ry_s.at[k], ry_r.at[k], pair).wait_recv()
            same(dst.at[upper], rx_s.at[k], rx_r.at[k], pair).wait_recv()
            give(dx, dy)
    for dx in range(NX):
        for dy in range(NY):
            hand_on(1 - c, dx, dy).wait_recv()
    for cp in sends:
        cp.wait_send()


def body(hidden_acts, out_grads, momentum, weight_tiles, kept_ids, kept_counts):
    hbm = pl.BlockSpec(memory_space=pltpu.HBM)
    vmem = pl.BlockSpec(memory_space=pltpu.VMEM)

    def both(*shape):
        return [pltpu.VMEM(shape, BF16)] * 2

    def pairs(*counts):
        return [pltpu.SemaphoreType.DMA((n,)) for n in counts for _ in range(2)]

    dma = pltpu.SemaphoreType.DMA
    gathered, moment_out = pl.pallas_call(
        kernel,
        out_shape=(
            jax.ShapeDtypeStruct((NX, NY, 2, ROWS, 128), BF16),
            jax.ShapeDtypeStruct((ROWS, 128), F32),
        ),
        in_specs=[hbm] * 7,
        out_specs=(vmem, vmem),
        scratch_shapes=[
            pltpu.VMEM((256, 128), BF16),
            pltpu.VMEM((PARTS, 256, PART_COLS), BF16),
            pltpu.VMEM((ROWS, 128), F32),
            pltpu.VMEM((3, TILE_SQ), BF16),
            pltpu.SMEM((3, 1, 4), jnp.int32),
            pltpu.SMEM((1, 3), jnp.int32),
            pltpu.VMEM((448, 128), F32),
            pltpu.VMEM((2, NX, NY, ROWS, 128), BF16),
            pltpu.VMEM((NX, NY, ROWS, 128), BF16),
            pltpu.VMEM((ROWS, 128), F32),
            pltpu.VMEM((NZ, 16, 128), BF16),
            pltpu.VMEM((ROWS, 128), F32),
            pltpu.VMEM((NX, Y_ROWS, 128), F32),
            pltpu.VMEM((NY, ROWS - Y_ROWS, 128), F32),
            *both(NY - 1, NX, Y_ROWS, 128),
            *both(NX - 1, NY, ROWS - Y_ROWS, 128),
            *both(NY - 1, ROWS - Y_ROWS, 128),
            *both(NX - 1, Y_ROWS, 128),
            dma((PARTS,)),
            dma((6,)),
            *pairs(2 * PARTS, 7, 3, 7, 3, 7, 7, 3, 21, 21, 32),
        ],
        compiler_params=pltpu.CompilerParams(
            collective_id=0, has_side_effects=True, vmem_limit_bytes=56 * 1024 * 1024
        ),
    )(
        hidden_acts, out_grads, momentum.reshape(ROWS, 128), weight_tiles,
        kept_ids.transpose(1, 0, 2), kept_counts, jnp.asarray(constants()),
    )
    return gathered.reshape(192, TILE_SQ), moment_out.reshape(1, 3, TILE_SQ)


def solution(mesh):
    in_specs = (
        P("rep", "shard", None),
        P("rep", "shard", None),
        P("rep", "shard", None),
        P("shard", None),
        P("rep", "shard", None),
        P("rep", "shard"),
    )
    out_specs = (P(), P("rep", "shard", None))
    return jax.shard_map(body, mesh=mesh, in_specs=in_specs, out_specs=out_specs, check_vma=False)
```

time: 81.9 us -> 60 us (0.73)
  Pallas kernels: 71.6 us -> 54.9 us
  local copies, waits for them, and re-layouts: 9.32 us -> 4.32 us
    pallas_call x1, Pallas kernels: 71.6 us -> 54.9 us  [body(): pl.pallas_call(kernel, out_shape=(jax.ShapeDtypeStruct((NX, NY, 2, ROWS,...]
    unnamed x13 -> x3, local copies, waits for them, and re-layouts: 7.26 us -> 0.62 us
    reshape x1, local copies, waits for them, and re-layouts: 2.06 us -> 3.69 us  [body(): return (gathered.reshape(192, TILE_SQ), moment_out.reshape(1, 3, TILE_SQ))]
where the time goes in v2:
time: 60 us; the launch traced here: 59.9 us
  Pallas kernels  54.9 us (92%)
  local copies, waits for them, and re-layouts  4.32 us (7%)
  between operations  0.65 us (1%)
    pallas_call x1, Pallas kernels, body(): pl.pallas_call(kernel, out_shape=(jax.ShapeDtypeStruct((NX, NY, 2, ROWS,...  54.9 us
    reshape x1, local copies, waits for them, and re-layouts, body(): return (gathered.reshape(192, TILE_SQ), moment_out.reshape(1, 3, TILE_SQ))  3.69 us

profile of v2, /device:TPU:1, one launch (start us, length us, event | category | flops | bytes accessed | tf_op | source)
XLA Modules:
  0.0 59.9 jit_solution(11615804780620119196)
XLA Ops:
  0.6 54.9 %shard_map.86 = (bf16[4,8,2,96,128]{4,3,2,1,0:T(8,128)(2,1)}, f32[96,128]{1,0:T(8,128)}) custom-call(bf16[1,256,128]{2,1,0:T(8,128)(2,1)} %hid.1, bf16[1,256,6144]{2,1,0:T(8,128)(2,1)} %grads.1, f32[96,128]{1,0:T(8,128)} %bitcast.6, bf16[3,4096]{1,0:T(4,128)(2,1)} %wts.1, s32[3,1,4]{2,1,0:T(1,128)} %bitcast.7, s32[1,3]{1,0:T(1,128)} %counts.1, ...), custom_call_target="tpu_custom_call" | custom-call | tf_op jit(solution)/shard_map/pallas_call | solution.py:390
  55.5 0.0 copy-start
  55.6 3.7 %reshape.14 = bf16[192,4096]{1,0:T(8,128)(2,1)} reshape(bf16[4,8,2,96,128]{4,3,2,1,0:T(8,128)(2,1)} %get-tuple-element.4) | data formatting | bytes 3145728 | tf_op jit(solution)/shard_map/reshape | solution.py:428
  59.2 0.0 copy-done
  59.3 0.6 %copy.12 = f32[1,3,4096]{2,0,1:T(1,128)} copy(f32[1,3,4096]{2,0,1:T(1,128)S(1)} %bitcast.5) | data formatting | bytes 98304
Async XLA Ops:
  55.5 3.7 %copy-start = (f32[96,128]{1,0:T(8,128)S(1)}, f32[96,128]{1,0:T(8,128)}, u32[]{:S(2)}) copy-start(f32[96,128]{1,0:T(8,128)} %get-tuple-element.5) | copy-start | bytes 147460

commit v3 on v2

--- a/solution.py
+++ b/solution.py
@@ -16,12 +16,12 @@
 ROWS = 96
 Y_ROWS = 32
 G_ROWS = 32
-X_NEAR = (1, 3, 2)
-Y_NEAR = (1, 7, 2, 6, 3, 5, 4)
+X_FAR = (2, 1, 3)
+Y_FAR = (4, 3, 5, 2, 6, 1, 7)
+X_PARTS = 2
 PARTS = 4
 PART_COLS = D // PARTS
 PART_CHIPS = PART_COLS // 384
-BARRIER_AT = 3
 MOMENTUM_DECAY = 0.9
 STEP = 2.0 / 8.0
 GRAD_SCALE = 1.0 / 128.0
@@ -57,8 +57,8 @@
 
 def kernel(
     hid, grads, mom, wts, ids, counts, consts,
-    gath, mom_out,
-    hid_v, gbuf, mom_v, wts_v, ids_v, counts_v, consts_v,
+    out, mom_out,
+    gath, rows_f, hid_v, gbuf, mom_v, wts_v, ids_v, counts_v, consts_v,
     part, prx, wsum, zbuf, slab, acc_y, acc_x,
     st_y1, rx_y1, st_x1, rx_x1, st_y2, rx_y2, st_x2, rx_x2,
     load_sem, in_sem, pair_s, pair_r,
@@ -93,7 +93,7 @@
 
     pair = dev(x, y, 1 - c)
     barrier = pltpu.get_barrier_semaphore()
-    partners = [pair] + [to_x(d) for d in X_NEAR] + [to_y(d) for d in Y_NEAR]
+    partners = [pair] + [to_x(d) for d in X_FAR] + [to_y(d) for d in Y_FAR]
     partners += [(shard, (z + d) % NZ) for d in range(1, NZ)]
     for who in partners:
         pl.semaphore_signal(barrier, inc=1, device_id=who, device_id_type=MESH)
@@ -124,7 +124,6 @@
     ).astype(BF16)
 
     left = iota((32, 128), 1) < 64
-    pair_copies = []
     for p in range(PARTS):
         loads[p].wait()
         full = jnp.dot(hid_t, gbuf[p], preferred_element_type=F32)
@@ -140,70 +139,77 @@
                     for t, val in ((2 * b, first), (2 * b + 1, second)):
                         row = (t % 3) * 32
                         part[t // 3, chip // 8, chip % 8, row:row + 32, :] = val
-        if p == BARRIER_AT:
-            pl.semaphore_wait(barrier, len(partners))
-        for i in range(2):
-            lo = (i * 16 + p * PART_CHIPS) // 8
-            yy = (p * PART_CHIPS) % 8
-            cp = pltpu.make_async_remote_copy(
-                src_ref=part.at[1 - c, lo, pl.ds(yy, PART_CHIPS)],
-                dst_ref=prx.at[lo, pl.ds(yy, PART_CHIPS)],
-                send_sem=pair_s.at[p * 2 + i],
-                recv_sem=pair_r.at[p * 2 + i],
-                device_id=pair,
-                device_id_type=MESH,
-            )
-            pair_copies.append(cp)
-        if p >= BARRIER_AT:
-            for cp in pair_copies[0 if p == BARRIER_AT else -2:]:
-                cp.start()
-    for cp in pair_copies:
-        cp.wait()
-
+    pl.semaphore_wait(barrier, len(partners))
+
+    ys, xs = slice(0, Y_ROWS), slice(Y_ROWS, ROWS)
+    every = slice(None)
+    y_rows, x_rows = pl.ds(0, Y_ROWS), pl.ds(Y_ROWS, ROWS - Y_ROWS)
+    pair_copies = []
+    for k, ix in enumerate(
+        [(x_at(d), every, x_rows) for d in X_FAR] + [(every, every, y_rows), (x, every, x_rows)]
+    ):
+        cp = remote(part.at[(1 - c,) + ix], prx.at[ix], pair_s.at[k], pair_r.at[k], pair)
+        cp.start()
+        pair_copies.append(cp)
 
     def own(ix):
         return part[(c,) + ix].astype(F32) + prx[ix].astype(F32)
 
-    ys, xs = slice(0, Y_ROWS), slice(Y_ROWS, ROWS)
-    every = slice(None)
     first_x, first_y, second_y, second_x = [], [], [], []
-    for d in X_NEAR:
-        st_x1[d - 1] = own((x_at(d), every, xs)).astype(BF16)
-        cp = remote(st_x1.at[d - 1], rx_x1.at[d - 1], x1_s.at[d - 1], x1_r.at[d - 1], to_x(d))
-        cp.start()
-        first_x.append(cp)
-    for d in Y_NEAR:
-        st_y1[d - 1] = own((every, y_at(d), ys)).astype(BF16)
-        cp = remote(st_y1.at[d - 1], rx_y1.at[d - 1], y1_s.at[d - 1], y1_r.at[d - 1], to_y(d))
-        cp.start()
-        first_y.append(cp)
-    total = own((x, every, xs))
-    for cp, d in zip(first_x, X_NEAR):
-        cp.wait_recv()
-        total = total + rx_x1[d - 1].astype(F32)
-    acc_x[...] = total
-    for d in Y_NEAR:
-        st_y2[d - 1] = acc_x[y_at(d)].astype(BF16)
-        cp = remote(st_y2.at[d - 1], rx_y2.at[d - 1], y2_s.at[d - 1], y2_r.at[d - 1], to_y(d))
-        cp.start()
-        second_y.append(cp)
+    order = Y_FAR + (0,)
+    step = NY // X_PARTS
+    for part_no in range(X_PARTS):
+        ks = range(part_no * step, (part_no + 1) * step)
+        for i, d in enumerate(X_FAR):
+            if part_no == 0:
+                pair_copies[i].wait_recv()
+            for k in ks:
+                st_x1[d - 1, k] = own((x_at(d), y_at(order[k]), xs)).astype(BF16)
+            at = pl.ds(part_no * step, step)
+            n = (d - 1) * X_PARTS + part_no
+            cp = remote(st_x1.at[d - 1, at], rx_x1.at[d - 1, at], x1_s.at[n], x1_r.at[n], to_x(d))
+            cp.start()
+            first_x.append(cp)
+        if part_no == 0:
+            pair_copies[3].wait_recv()
+            for d in Y_FAR:
+                st_y1[d - 1] = own((every, y_at(d), ys)).astype(BF16)
+                cp = remote(st_y1.at[d - 1], rx_y1.at[d - 1], y1_s.at[d - 1], y1_r.at[d - 1], to_y(d))
+                cp.start()
+                first_y.append(cp)
+    pair_copies[4].wait_recv()
+    for part_no in range(X_PARTS):
+        for cp in first_x[3 * part_no:3 * part_no + 3]:
+            cp.wait_recv()
+        for k in range(part_no * step, (part_no + 1) * step):
+            total = own((x, y_at(order[k]), xs))
+            for d in X_FAR:
+                total = total + rx_x1[d - 1, k].astype(F32)
+            d = order[k]
+            if d == 0:
+                acc_x[...] = total
+                continue
+            st_y2[d - 1] = total.astype(BF16)
+            cp = remote(st_y2.at[d - 1], rx_y2.at[d - 1], y2_s.at[d - 1], y2_r.at[d - 1], to_y(d))
+            cp.start()
+            second_y.append(cp)
     total = own((every, y, ys))
-    for cp, d in zip(first_y, Y_NEAR):
+    for cp, d in zip(first_y, Y_FAR):
         cp.wait_recv()
         total = total + rx_y1[d - 1].astype(F32)
     acc_y[...] = total
-    for d in X_NEAR:
+    for d in X_FAR:
         st_x2[d - 1] = acc_y[x_at(d)].astype(BF16)
         cp = remote(st_x2.at[d - 1], rx_x2.at[d - 1], x2_s.at[d - 1], x2_r.at[d - 1], to_x(d))
         cp.start()
         second_x.append(cp)
-    total = acc_x[y]
-    for cp, d in zip(second_y, Y_NEAR):
+    total = acc_x[...]
+    for cp, d in zip(second_y, Y_FAR):
         cp.wait_recv()
         total = total + rx_y2[d - 1].astype(F32)
     slab[xs] = total
     total = acc_y[x]
-    for cp, d in zip(second_x, X_NEAR):
+    for cp, d in zip(second_x, X_FAR):
         cp.wait_recv()
         total = total + rx_x2[d - 1].astype(F32)
     slab[ys] = total
@@ -318,18 +324,18 @@
     gath[x, y, c] = (wsum[...] - STEP * update).astype(BF16)
 
 
-    sends += first_x + first_y + second_x + second_y
+    sends += pair_copies + first_x + first_y + second_x + second_y
     lower, upper = pl.ds(0, G_ROWS), pl.ds(G_ROWS, ROWS - G_ROWS)
 
     def same(ref, send, recv, who):
         return remote(ref, ref, send, recv, who)
 
     mine = gath.at[x, y, c]
-    for d in X_NEAR:
+    for d in X_FAR:
         cp = same(mine, gx_s.at[d - 1], gx_r.at[d - 1], to_x(d))
         cp.start()
         sends.append(cp)
-    for d in Y_NEAR:
+    for d in Y_FAR:
         cp = same(mine, gy_s.at[d - 1], gy_r.at[d - 1], to_y(d))
         cp.start()
         sends.append(cp)
@@ -338,40 +344,56 @@
         k = dx * NY + dy
         return same(gath.at[x_at(NX - dx), y_at(NY - dy), cc], fw_s.at[k], fw_r.at[k], pair)
 
+    def place(cc, dx, dy):
+        xx, yy = x_at(NX - dx), y_at(NY - dy)
+        tile = ((xx * NY + yy) * 2 + cc) * 3
+        val = gath[xx, yy, cc].astype(F32)
+        for k in range(3):
+            rows_f[pl.ds(tile + k, 32, stride=192), :] = val[k * 32:(k + 1) * 32]
+
     def give(dx, dy):
         cp = hand_on(c, dx, dy)
         cp.start()
         sends.append(cp)
 
     give(0, 0)
-    for dx in X_NEAR:
+    place(c, 0, 0)
+    for dx in X_FAR:
         src = gath.at[x_at(NX - dx), y, c]
         same(src, gx_s.at[dx - 1], gx_r.at[dx - 1], pair).wait_recv()
-        for dy in Y_NEAR:
+        for dy in Y_FAR:
             k = (dx - 1) * 7 + dy - 1
             cp = same(src.at[lower], ry_s.at[k], ry_r.at[k], to_y(dy))
             cp.start()
             sends.append(cp)
         give(dx, 0)
-    for dy in Y_NEAR:
+        place(c, dx, 0)
+    for dy in Y_FAR:
         src = gath.at[x, y_at(NY - dy), c]
         same(src, gy_s.at[dy - 1], gy_r.at[dy - 1], pair).wait_recv()
-        for dx in X_NEAR:
+        for dx in X_FAR:
             k = (dx - 1) * 7 + dy - 1
             cp = same(src.at[upper], rx_s.at[k], rx_r.at[k], to_x(dx))
             cp.start()
             sends.append(cp)
         give(0, dy)
-    for dy in Y_NEAR:
-        for dx in X_NEAR:
+        place(c, 0, dy)
+    for dy in Y_FAR:
+        for dx in X_FAR:
             k = (dx - 1) * 7 + dy - 1
             dst = gath.at[x_at(NX - dx), y_at(NY - dy), c]
             same(dst.at[lower], ry_s.at[k], ry_r.at[k], pair).wait_recv()
             same(dst.at[upper], rx_s.at[k], rx_r.at[k], pair).wait_recv()
             give(dx, dy)
-    for dx in range(NX):
-        for dy in range(NY):
-            hand_on(1 - c, dx, dy).wait_recv()
+            place(c, dx, dy)
+    for dx, dy in (
+        [(0, 0)] + [(d, 0) for d in X_FAR] + [(0, d) for d in Y_FAR]
+        + [(dx, dy) for dy in Y_FAR for dx in X_FAR]
+    ):
+        hand_on(1 - c, dx, dy).wait_recv()
+        place(1 - c, dx, dy)
+    for m in range(32):
+        out[:, m * 128:(m + 1) * 128] = rows_f[m * 192:(m + 1) * 192].astype(BF16)
     for cp in sends:
         cp.wait_send()
 
@@ -390,12 +412,14 @@
     gathered, moment_out = pl.pallas_call(
         kernel,
         out_shape=(
-            jax.ShapeDtypeStruct((NX, NY, 2, ROWS, 128), BF16),
+            jax.ShapeDtypeStruct((192, TILE_SQ), BF16),
             jax.ShapeDtypeStruct((ROWS, 128), F32),
         ),
         in_specs=[hbm] * 7,
         out_specs=(vmem, vmem),
         scratch_shapes=[
+            pltpu.VMEM((NX, NY, 2, ROWS, 128), BF16),
+            pltpu.VMEM((32 * 192, 128), F32),
             pltpu.VMEM((256, 128), BF16),
             pltpu.VMEM((PARTS, 256, PART_COLS), BF16),
             pltpu.VMEM((ROWS, 128), F32),
@@ -409,23 +433,26 @@
             pltpu.VMEM((NZ, 16, 128), BF16),
             pltpu.VMEM((ROWS, 128), F32),
             pltpu.VMEM((NX, Y_ROWS, 128), F32),
-            pltpu.VMEM((NY, ROWS - Y_ROWS, 128), F32),
+            pltpu.VMEM((ROWS - Y_ROWS, 128), F32),
             *both(NY - 1, NX, Y_ROWS, 128),
             *both(NX - 1, NY, ROWS - Y_ROWS, 128),
             *both(NY - 1, ROWS - Y_ROWS, 128),
             *both(NX - 1, Y_ROWS, 128),
             dma((PARTS,)),
             dma((6,)),
-            *pairs(2 * PARTS, 7, 3, 7, 3, 7, 7, 3, 21, 21, 32),
+            *pairs(5, 7, 3 * X_PARTS, 7, 3, 7, 7, 3, 21, 21, 32),
         ],
         compiler_params=pltpu.CompilerParams(
-            collective_id=0, has_side_effects=True, vmem_limit_bytes=56 * 1024 * 1024
+            collective_id=0, has_side_effects=True, vmem_limit_bytes=48 * 1024 * 1024
         ),
-    )(
-        hidden_acts, out_grads, momentum.reshape(ROWS, 128), weight_tiles,
-        kept_ids.transpose(1, 0, 2), kept_counts, jnp.asarray(constants()),
-    )
-    return gathered.reshape(192, TILE_SQ), moment_out.reshape(1, 3, TILE_SQ)
+    )(*(
+        pltpu.with_memory_space_constraint(arg, pltpu.HBM)
+        for arg in (
+            hidden_acts, out_grads, momentum.reshape(ROWS, 128), weight_tiles,
+            kept_ids.transpose(1, 0, 2), kept_counts, jnp.asarray(constants()),
+        )
+    ))
+    return gathered, moment_out.reshape(1, 3, TILE_SQ)
 
 
 def solution(mesh):

time: 60 us -> 52.8 us (0.88)
  Pallas kernels: 54.9 us -> 50.3 us
  local copies, waits for them, and re-layouts: 4.32 us -> 1.76 us
    pallas_call x1, Pallas kernels: 54.9 us -> 50.3 us  [body(): pl.pallas_call(kernel, out_shape=(jax.ShapeDtypeStruct((192, TILE_SQ), BF...]
    reshape x1 -> x0, local copies, waits for them, and re-layouts: 3.69 us -> none  [body(): return (gathered.reshape(192, TILE_SQ), moment_out.reshape(1, 3, TILE_SQ))]
    unnamed x3 -> x2, local copies, waits for them, and re-layouts: 0.62 us -> 1.76 us
where the time goes in v3:
time: 52.8 us; the launch traced here: 52.7 us
  Pallas kernels  50.3 us (95%)
  local copies, waits for them, and re-layouts  1.76 us (3%)
  between operations  0.64 us (1%)
    pallas_call x1, Pallas kernels, body(): pl.pallas_call(kernel, out_shape=(jax.ShapeDtypeStruct((192, TILE_SQ), BF...  50.3 us
    unnamed x2, local copies, waits for them, and re-layouts  1.76 us

profile of v3, /device:TPU:1, one launch (start us, length us, event | category | flops | bytes accessed | tf_op | source)
XLA Modules:
  0.0 52.7 jit_solution(1876982982479423277)
XLA Ops:
  0.6 50.3 %shard_map.86 = (bf16[192,4096]{1,0:T(8,128)(2,1)S(1)}, f32[96,128]{1,0:T(8,128)S(1)}) custom-call(bf16[1,256,128]{2,1,0:T(8,128)(2,1)} %hid.1, bf16[1,256,6144]{2,1,0:T(8,128)(2,1)} %grads.1, f32[96,128]{1,0:T(8,128)} %bitcast.4, bf16[3,4096]{1,0:T(4,128)(2,1)} %wts.1, s32[3,1,4]{2,1,0:T(1,128)} %bitcast.5, s32[1,3]{1,0:T(1,128)} %counts.1, ...), custom_call_target="tpu_custom_call" | custom-call | tf_op jit(solution)/shard_map/pallas_call | solution.py:412
  50.9 1.1 %copy.13 = bf16[192,4096]{1,0:T(8,128)(2,1)} copy(bf16[192,4096]{1,0:T(8,128)(2,1)S(1)} %get-tuple-element.12) | data formatting | bytes 3145728
  52.1 0.6 %copy.14 = f32[1,3,4096]{2,0,1:T(1,128)} copy(f32[1,3,4096]{2,0,1:T(1,128)S(1)} %bitcast.3) | data formatting | bytes 98304

commit v4 on v3

--- a/solution.py
+++ b/solution.py
@@ -18,6 +18,8 @@
 G_ROWS = 32
 X_FAR = (2, 1, 3)
 Y_FAR = (4, 3, 5, 2, 6, 1, 7)
+OFFSETS = (0,) + Y_FAR
+K_GROUPS = ((1, 3), (3, 5), (5, 8))
 X_PARTS = 2
 PARTS = 4
 PART_COLS = D // PARTS
@@ -153,7 +155,7 @@
         pair_copies.append(cp)
 
     def own(ix):
-        return part[(c,) + ix].astype(F32) + prx[ix].astype(F32)
+        return part[(c,) + ix] + prx[ix]
 
     first_x, first_y, second_y, second_x = [], [], [], []
     order = Y_FAR + (0,)
@@ -164,7 +166,7 @@
             if part_no == 0:
                 pair_copies[i].wait_recv()
             for k in ks:
-                st_x1[d - 1, k] = own((x_at(d), y_at(order[k]), xs)).astype(BF16)
+                st_x1[d - 1, k] = own((x_at(d), y_at(order[k]), xs))
             at = pl.ds(part_no * step, step)
             n = (d - 1) * X_PARTS + part_no
             cp = remote(st_x1.at[d - 1, at], rx_x1.at[d - 1, at], x1_s.at[n], x1_r.at[n], to_x(d))
@@ -173,7 +175,7 @@
         if part_no == 0:
             pair_copies[3].wait_recv()
             for d in Y_FAR:
-                st_y1[d - 1] = own((every, y_at(d), ys)).astype(BF16)
+                st_y1[d - 1] = own((every, y_at(d), ys))
                 cp = remote(st_y1.at[d - 1], rx_y1.at[d - 1], y1_s.at[d - 1], y1_r.at[d - 1], to_y(d))
                 cp.start()
                 first_y.append(cp)
@@ -182,7 +184,7 @@
         for cp in first_x[3 * part_no:3 * part_no + 3]:
             cp.wait_recv()
         for k in range(part_no * step, (part_no + 1) * step):
-            total = own((x, y_at(order[k]), xs))
+            total = own((x, y_at(order[k]), xs)).astype(F32)
             for d in X_FAR:
                 total = total + rx_x1[d - 1, k].astype(F32)
             d = order[k]
@@ -193,7 +195,7 @@
             cp = remote(st_y2.at[d - 1], rx_y2.at[d - 1], y2_s.at[d - 1], y2_r.at[d - 1], to_y(d))
             cp.start()
             second_y.append(cp)
-    total = own((every, y, ys))
+    total = own((every, y, ys)).astype(F32)
     for cp, d in zip(first_y, Y_FAR):
         cp.wait_recv()
         total = total + rx_y1[d - 1].astype(F32)
@@ -321,77 +323,72 @@
                 total = total + jnp.where(unitf == num, val, 0.0)
         totals.append(total)
     update = inverse(jnp.concatenate(totals, axis=0))
-    gath[x, y, c] = (wsum[...] - STEP * update).astype(BF16)
+    gath[x, 0, c] = (wsum[...] - STEP * update).astype(BF16)
 
 
     sends += pair_copies + first_x + first_y + second_x + second_y
     lower, upper = pl.ds(0, G_ROWS), pl.ds(G_ROWS, ROWS - G_ROWS)
 
-    def same(ref, send, recv, who):
-        return remote(ref, ref, send, recv, who)
-
-    mine = gath.at[x, y, c]
+    def go(src, dst, send, recv, who):
+        cp = remote(src, dst, send, recv, who)
+        cp.start()
+        sends.append(cp)
+
+    def got(dst, send, recv):
+        remote(dst, dst, send, recv, pair).wait_recv()
+
+    def place(cc, i, k):
+        tile = ((i * NY + y_at(NY - OFFSETS[k])) * 2 + cc) * 3
+        val = gath[i, k, cc].astype(F32)
+        for t in range(3):
+            rows_f[pl.ds(tile + t, 32, stride=192), :] = val[t * 32:(t + 1) * 32]
+
+    def slabs(cc, lo, hi):
+        return gath.at[:, pl.ds(lo, hi - lo), cc]
+
     for d in X_FAR:
-        cp = same(mine, gx_s.at[d - 1], gx_r.at[d - 1], to_x(d))
-        cp.start()
-        sends.append(cp)
-    for d in Y_FAR:
-        cp = same(mine, gy_s.at[d - 1], gy_r.at[d - 1], to_y(d))
-        cp.start()
-        sends.append(cp)
-
-    def hand_on(cc, dx, dy):
-        k = dx * NY + dy
-        return same(gath.at[x_at(NX - dx), y_at(NY - dy), cc], fw_s.at[k], fw_r.at[k], pair)
-
-    def place(cc, dx, dy):
-        xx, yy = x_at(NX - dx), y_at(NY - dy)
-        tile = ((xx * NY + yy) * 2 + cc) * 3
-        val = gath[xx, yy, cc].astype(F32)
-        for k in range(3):
-            rows_f[pl.ds(tile + k, 32, stride=192), :] = val[k * 32:(k + 1) * 32]
-
-    def give(dx, dy):
-        cp = hand_on(c, dx, dy)
-        cp.start()
-        sends.append(cp)
-
-    give(0, 0)
-    place(c, 0, 0)
-    for dx in X_FAR:
-        src = gath.at[x_at(NX - dx), y, c]
-        same(src, gx_s.at[dx - 1], gx_r.at[dx - 1], pair).wait_recv()
-        for dy in Y_FAR:
-            k = (dx - 1) * 7 + dy - 1
-            cp = same(src.at[lower], ry_s.at[k], ry_r.at[k], to_y(dy))
-            cp.start()
-            sends.append(cp)
-        give(dx, 0)
-        place(c, dx, 0)
-    for dy in Y_FAR:
-        src = gath.at[x, y_at(NY - dy), c]
-        same(src, gy_s.at[dy - 1], gy_r.at[dy - 1], pair).wait_recv()
-        for dx in X_FAR:
-            k = (dx - 1) * 7 + dy - 1
-            cp = same(src.at[upper], rx_s.at[k], rx_r.at[k], to_x(dx))
-            cp.start()
-            sends.append(cp)
-        give(0, dy)
-        place(c, 0, dy)
-    for dy in Y_FAR:
-        for dx in X_FAR:
-            k = (dx - 1) * 7 + dy - 1
-            dst = gath.at[x_at(NX - dx), y_at(NY - dy), c]
-            same(dst.at[lower], ry_s.at[k], ry_r.at[k], pair).wait_recv()
-            same(dst.at[upper], rx_s.at[k], rx_r.at[k], pair).wait_recv()
-            give(dx, dy)
-            place(c, dx, dy)
-    for dx, dy in (
-        [(0, 0)] + [(d, 0) for d in X_FAR] + [(0, d) for d in Y_FAR]
-        + [(dx, dy) for dy in Y_FAR for dx in X_FAR]
-    ):
-        hand_on(1 - c, dx, dy).wait_recv()
-        place(1 - c, dx, dy)
+        mine = gath.at[x, 0, c]
+        go(mine, mine, gx_s.at[d - 1], gx_r.at[d - 1], to_x(d))
+    for k in range(1, NY):
+        go(
+            gath.at[x, 0, c, upper], gath.at[x, k, c, upper], gy_s.at[k - 1], gy_r.at[k - 1],
+            to_y(OFFSETS[k]),
+        )
+    for d in X_FAR:
+        got(gath.at[x_at(NX - d), 0, c], gx_s.at[d - 1], gx_r.at[d - 1])
+    for k in range(1, NY):
+        go(
+            gath.at[:, 0, c, lower], gath.at[:, k, c, lower], ry_s.at[k - 1], ry_r.at[k - 1],
+            to_y(OFFSETS[k]),
+        )
+    go(slabs(c, 0, 1), slabs(c, 0, 1), fw_s.at[0], fw_r.at[0], pair)
+    for i in range(NX):
+        place(c, i, 0)
+    for n, (lo, hi) in enumerate(K_GROUPS):
+        for k in range(lo, hi):
+            got(gath.at[x, k, c, upper], gy_s.at[k - 1], gy_r.at[k - 1])
+        for d in X_FAR:
+            ref = gath.at[x, pl.ds(lo, hi - lo), c, upper]
+            m = n * 3 + d - 1
+            go(ref, ref, rx_s.at[m], rx_r.at[m], to_x(d))
+    got(slabs(1 - c, 0, 1), fw_s.at[0], fw_r.at[0])
+    for i in range(NX):
+        place(1 - c, i, 0)
+    for n, (lo, hi) in enumerate(K_GROUPS):
+        for k in range(lo, hi):
+            got(gath.at[:, k, c, lower], ry_s.at[k - 1], ry_r.at[k - 1])
+        for d in X_FAR:
+            m = n * 3 + d - 1
+            got(gath.at[x_at(NX - d), pl.ds(lo, hi - lo), c, upper], rx_s.at[m], rx_r.at[m])
+        go(slabs(c, lo, hi), slabs(c, lo, hi), fw_s.at[n + 1], fw_r.at[n + 1], pair)
+        for k in range(lo, hi):
+            for i in range(NX):
+                place(c, i, k)
+    for n, (lo, hi) in enumerate(K_GROUPS):
+        got(slabs(1 - c, lo, hi), fw_s.at[n + 1], fw_r.at[n + 1])
+        for k in range(lo, hi):
+            for i in range(NX):
+                place(1 - c, i, k)
     for m in range(32):
         out[:, m * 128:(m + 1) * 128] = rows_f[m * 192:(m + 1) * 192].astype(BF16)
     for cp in sends:
@@ -440,7 +437,7 @@
             *both(NX - 1, Y_ROWS, 128),
             dma((PARTS,)),
             dma((6,)),
-            *pairs(5, 7, 3 * X_PARTS, 7, 3, 7, 7, 3, 21, 21, 32),
+            *pairs(5, 7, 3 * X_PARTS, 7, 3, 7, 7, 3, 7, 3 * len(K_GROUPS), 1 + len(K_GROUPS)),
         ],
         compiler_params=pltpu.CompilerParams(
             collective_id=0, has_side_effects=True, vmem_limit_bytes=48 * 1024 * 1024

time: 52.8 us -> 51.7 us (0.979)
  Pallas kernels: 50.3 us -> 49.1 us
    pallas_call x1, Pallas kernels: 50.3 us -> 49.1 us  [body(): pl.pallas_call(kernel, out_shape=(jax.ShapeDtypeStruct((192, TILE_SQ), BF...]
where the time goes in v4:
time: 51.7 us; the launch traced here: 51.5 us
  Pallas kernels  49.1 us (95%)
  local copies, waits for them, and re-layouts  1.76 us (3%)
  between operations  0.64 us (1%)
    pallas_call x1, Pallas kernels, body(): pl.pallas_call(kernel, out_shape=(jax.ShapeDtypeStruct((192, TILE_SQ), BF...  49.1 us
    unnamed x2, local copies, waits for them, and re-layouts  1.76 us

profile of v4, /device:TPU:1, one launch (start us, length us, event | category | flops | bytes accessed | tf_op | source)
XLA Modules:
  0.0 51.5 jit_solution(12919007984638221074)
XLA Ops:
  0.6 49.1 %shard_map.86 = (bf16[192,4096]{1,0:T(8,128)(2,1)S(1)}, f32[96,128]{1,0:T(8,128)S(1)}) custom-call(bf16[1,256,128]{2,1,0:T(8,128)(2,1)} %hid.1, bf16[1,256,6144]{2,1,0:T(8,128)(2,1)} %grads.1, f32[96,128]{1,0:T(8,128)} %bitcast.4, bf16[3,4096]{1,0:T(4,128)(2,1)} %wts.1, s32[3,1,4]{2,1,0:T(1,128)} %bitcast.5, s32[1,3]{1,0:T(1,128)} %counts.1, ...), custom_call_target="tpu_custom_call" | custom-call | tf_op jit(solution)/shard_map/pallas_call | solution.py:409
  49.8 1.1 %copy.13 = bf16[192,4096]{1,0:T(8,128)(2,1)} copy(bf16[192,4096]{1,0:T(8,128)(2,1)S(1)} %get-tuple-element.12) | data formatting | bytes 3145728
  50.9 0.6 %copy.14 = f32[1,3,4096]{2,0,1:T(1,128)} copy(f32[1,3,4096]{2,0,1:T(1,128)S(1)} %bitcast.3) | data formatting | bytes 98304

commit v5 on v4

--- a/solution.py
+++ b/solution.py
@@ -48,9 +48,12 @@
 
 
 def dot32(a, b):
-    return lax.dot_general(
-        a, b, (((1,), (0,)), ((), ())), precision=lax.Precision.HIGHEST, preferred_element_type=F32
-    )
+    def dot(u, v):
+        return jnp.dot(u, v, preferred_element_type=F32)
+
+    a_hi, b_hi = a.astype(BF16), b.astype(BF16)
+    a_lo, b_lo = (a - a_hi.astype(F32)).astype(BF16), (b - b_hi.astype(F32)).astype(BF16)
+    return dot(a_hi, b_hi) + (dot(a_hi, b_lo) + dot(a_lo, b_hi))
 
 
 def iota(shape, dim):

time: 51.7 us -> 51.3 us (level)
  no operation moved by 1% of the time
where the time goes in v5:
time: 51.3 us; the launch traced here: 51.1 us
  Pallas kernels  48.7 us (95%)
  local copies, waits for them, and re-layouts  1.76 us (3%)
  between operations  0.64 us (1%)
    pallas_call x1, Pallas kernels, body(): pl.pallas_call(kernel, out_shape=(jax.ShapeDtypeStruct((192, TILE_SQ), BF...  48.7 us
    unnamed x2, local copies, waits for them, and re-layouts  1.76 us

profile of v5, /device:TPU:1, one launch (start us, length us, event | category | flops | bytes accessed | tf_op | source)
XLA Modules:
  0.0 51.1 jit_solution(14120668054769916537)
XLA Ops:
  0.6 48.7 %shard_map.86 = (bf16[192,4096]{1,0:T(8,128)(2,1)S(1)}, f32[96,128]{1,0:T(8,128)S(1)}) custom-call(bf16[1,256,128]{2,1,0:T(8,128)(2,1)} %hid.1, bf16[1,256,6144]{2,1,0:T(8,128)(2,1)} %grads.1, f32[96,128]{1,0:T(8,128)} %bitcast.4, bf16[3,4096]{1,0:T(4,128)(2,1)} %wts.1, s32[3,1,4]{2,1,0:T(1,128)} %bitcast.5, s32[1,3]{1,0:T(1,128)} %counts.1, ...), custom_call_target="tpu_custom_call" | custom-call | tf_op jit(solution)/shard_map/pallas_call | solution.py:412
  49.4 1.1 %copy.13 = bf16[192,4096]{1,0:T(8,128)(2,1)} copy(bf16[192,4096]{1,0:T(8,128)(2,1)S(1)} %get-tuple-element.12) | data formatting | bytes 3145728
  50.5 0.6 %copy.14 = f32[1,3,4096]{2,0,1:T(1,128)} copy(f32[1,3,4096]{2,0,1:T(1,128)S(1)} %bitcast.3) | data formatting | bytes 98304

commit v6 on v5

--- a/solution.py
+++ b/solution.py
@@ -329,7 +329,8 @@
     gath[x, 0, c] = (wsum[...] - STEP * update).astype(BF16)
 
 
-    sends += pair_copies + first_x + first_y + second_x + second_y
+    early = sends + pair_copies + first_x + first_y + second_x + second_y
+    sends = []
     lower, upper = pl.ds(0, G_ROWS), pl.ds(G_ROWS, ROWS - G_ROWS)
 
     def go(src, dst, send, recv, who):
@@ -357,6 +358,8 @@
             gath.at[x, 0, c, upper], gath.at[x, k, c, upper], gy_s.at[k - 1], gy_r.at[k - 1],
             to_y(OFFSETS[k]),
         )
+    for cp in early:
+        cp.wait_send()
     for d in X_FAR:
         got(gath.at[x_at(NX - d), 0, c], gx_s.at[d - 1], gx_r.at[d - 1])
     for k in range(1, NY):

time: 51.3 us -> 51.2 us (level)
  no operation moved by 1% of the time
where the time goes in v6:
time: 51.2 us; the launch traced here: 51.1 us
  Pallas kernels  48.7 us (95%)
  local copies, waits for them, and re-layouts  1.76 us (3%)
  between operations  0.64 us (1%)
    pallas_call x1, Pallas kernels, body(): pl.pallas_call(kernel, out_shape=(jax.ShapeDtypeStruct((192, TILE_SQ), BF...  48.7 us
    unnamed x2, local copies, waits for them, and re-layouts  1.76 us

profile of v6, /device:TPU:1, one launch (start us, length us, event | category | flops | bytes accessed | tf_op | source)
XLA Modules:
  0.0 51.1 jit_solution(9549299048472836582)
XLA Ops:
  0.6 48.7 %shard_map.86 = (bf16[192,4096]{1,0:T(8,128)(2,1)S(1)}, f32[96,128]{1,0:T(8,128)S(1)}) custom-call(bf16[1,256,128]{2,1,0:T(8,128)(2,1)} %hid.1, bf16[1,256,6144]{2,1,0:T(8,128)(2,1)} %grads.1, f32[96,128]{1,0:T(8,128)} %bitcast.4, bf16[3,4096]{1,0:T(4,128)(2,1)} %wts.1, s32[3,1,4]{2,1,0:T(1,128)} %bitcast.5, s32[1,3]{1,0:T(1,128)} %counts.1, ...), custom_call_target="tpu_custom_call" | custom-call | tf_op jit(solution)/shard_map/pallas_call | solution.py:415
  49.3 1.1 %copy.13 = bf16[192,4096]{1,0:T(8,128)(2,1)} copy(bf16[192,4096]{1,0:T(8,128)(2,1)S(1)} %get-tuple-element.12) | data formatting | bytes 3145728
  50.5 0.6 %copy.14 = f32[1,3,4096]{2,0,1:T(1,128)} copy(f32[1,3,4096]{2,0,1:T(1,128)S(1)} %bitcast.3) | data formatting | bytes 98304
